TPU v7x, 256 devices: a whole 4x4x8 slice. The times are simulated.
256 devices in a mesh: ctx: 32 (over z, y_hi, core), tp: 8 (over y_lo, x).
Axes of the slice: x: 4, y: 4 (y_hi: 2, y_lo: 2; y = y_hi * 2 + y_lo), z: 8, core: 2. Of those that a mesh axis runs over, the one named last changes fastest.
Arguments:
- queries: bfloat16 [8192, 4096], P('ctx', 'tp'), may hold values from -44 to 44
- keys: bfloat16 [8192, 1024], P('ctx', 'tp'), may hold values from -24 to 24
- values: bfloat16 [8192, 1024], P('ctx', 'tp'), may hold values from -6 to 6
- grad_out: bfloat16 [8192, 4096], P('ctx', 'tp'), may hold values from -6 to 6
- doc_lengths: int32 [17], replicated, may hold values from 1 to 4352, as said below
Outputs:
- grad_queries: bfloat16 [8192, 4096], P(('ctx', 'tp'))
- grad_keys: bfloat16 [8192, 1024], P(('ctx', 'tp'))
- grad_values: bfloat16 [8192, 1024], P(('ctx', 'tp'))
Inputs may be any that keep to these rules, and one draw needn't show every extreme that they name: `doc_lengths`: 17 documents fill the 8192 positions; the longest has exactly 4352 tokens.
All inputs are finite; a program needn't handle non-finite values.
Results may differ from a plain program's by a relative error of at most 0.008.
Values may be sent and summed in bfloat16 or wider, within the bound.
No kernel may reach another device: no remote copies, remote signals or barrier semaphores. Data moves between devices by JAX's collectives and lax.ppermute only.
A program may use at most 64 MiB of HBM per device.

v0:
```python
import jax
import jax.numpy as jnp
from jax import lax
from jax.sharding import PartitionSpec as P

HD = 128


NEG_FILL = -1e30


def row_starts(doc_lengths, positions):
    ends = jnp.cumsum(doc_lengths)
    before = (ends[None, :] <= positions[:, None]).astype(jnp.int32)
    return jnp.sum(before * doc_lengths[None, :], axis=1)


def tile_mask(query_pos, starts, key_first, width):
    key_pos = key_first + jnp.arange(width, dtype=jnp.int32)
    return (key_pos[None, :] >= starts[:, None]) & (key_pos[None, :] <= query_pos[:, None])


def stats_core(stats, block, mask, query_heads, grad_heads, scale):
    run_max, run_sum, run_dot = stats
    scores = (
        jnp.einsum("qhgd,khd->hgqk", query_heads, block[0], preferred_element_type=jnp.float32)
        * scale
    )
    filled = jnp.where(mask, scores, NEG_FILL)
    new_max = jnp.maximum(run_max, jnp.max(filled, axis=-1))
    weights = jnp.where(mask, jnp.exp(scores - new_max[..., None]), 0.0)
    grad_probs = jnp.einsum(
        "qhgd,khd->hgqk", grad_heads, block[1], preferred_element_type=jnp.float32
    )
    factor = jnp.exp(run_max - new_max)
    new_sum = run_sum * factor + jnp.sum(weights, axis=-1)
    new_dot = run_dot * factor + jnp.sum(weights * grad_probs, axis=-1)
    return (new_max, new_sum, new_dot)


def grad_core(block, mask, query_heads, grad_heads, lse, delta, scale):
    scores = (
        jnp.einsum("qhgd,khd->hgqk", query_heads, block[0], preferred_element_type=jnp.float32)
        * scale
    )
    probs = jnp.where(mask, jnp.exp(scores - lse[..., None]), 0.0)
    grad_probs = jnp.einsum(
        "qhgd,khd->hgqk", grad_heads, block[1], preferred_element_type=jnp.float32
    )
    grad_scores = probs * (grad_probs - delta[..., None])
    probs_b = probs.astype(jnp.bfloat16)
    grad_b = grad_scores.astype(jnp.bfloat16)
    query_add = jnp.einsum("hgqk,khd->qhgd", grad_b, block[0], preferred_element_type=jnp.float32)
    key_add = (
        jnp.einsum("hgqk,qhgd->khd", grad_b, query_heads, preferred_element_type=jnp.float32)
        * scale
    )
    value_add = jnp.einsum(
        "hgqk,qhgd->khd", probs_b, grad_heads, preferred_element_type=jnp.float32
    )
    return (query_add, jnp.stack((key_add, value_add)))


def local(queries, keys, values, grad_out, doc_lengths):
    rows = queries.shape[0]
    head_size = HD
    local_heads = keys.shape[1] // head_size
    group = queries.shape[1] // keys.shape[1]
    scale = head_size ** (-0.5)
    query_heads = queries.reshape(rows, local_heads, group, head_size)
    grad_heads = grad_out.reshape(rows, local_heads, group, head_size)
    kv_own = jnp.stack(
        (keys.reshape(rows, local_heads, head_size), values.reshape(rows, local_heads, head_size))
    )
    here = lax.axis_index("ctx")
    count = lax.axis_size("ctx")
    reach = count // 2 + 1
    query_pos = here * rows + jnp.arange(rows, dtype=jnp.int32)
    starts = row_starts(doc_lengths, query_pos)
    stat_shape = (local_heads, group, rows)
    stats_init = (
        jnp.full(stat_shape, NEG_FILL, jnp.float32),
        jnp.zeros(stat_shape, jnp.float32),
        jnp.zeros(stat_shape, jnp.float32),
    )
    query_zero = jnp.zeros((rows, local_heads, group, head_size), jnp.float32)

    def block_first(step):
        return (here - step) % count * rows

    def stats_at(step, stats, block):
        mask = tile_mask(query_pos, starts, block_first(step), rows)
        return lax.cond(
            jnp.any(mask),
            lambda s: stats_core(s, block, mask, query_heads, grad_heads, scale),
            lambda s: s,
            stats,
        )

    def grads_at(step, query_sum, kv_sum, block, lse, delta):
        mask = tile_mask(query_pos, starts, block_first(step), rows)

        def visit(carry):
            query_add, kv_add = grad_core(block, mask, query_heads, grad_heads, lse, delta, scale)
            return (carry[0] + query_add, carry[1] + kv_add)

        return lax.cond(jnp.any(mask), visit, lambda c: c, (query_sum, kv_sum))

    whole = lax.all_gather(kv_own, "ctx", axis=1, tiled=True)

    def piece_of(step):
        return lax.dynamic_slice_in_dim(whole, block_first(step), rows, 1)

    def stats_step(step, stats):
        return stats_at(step, stats, piece_of(step))

    stats = lax.fori_loop(0, reach + 1, stats_step, stats_init)
    lse = stats[0] + jnp.log(stats[1])
    delta = stats[2] / stats[1]

    def grads_step(step, carry):
        query_sum, kv_full = carry
        first = block_first(step)
        old = lax.dynamic_slice_in_dim(kv_full, first, rows, 1)
        query_sum, new = grads_at(step, query_sum, old, piece_of(step), lse, delta)
        return (query_sum, lax.dynamic_update_slice_in_dim(kv_full, new, first, 1))

    kv_zero = jnp.zeros((2, count * rows, local_heads, head_size), jnp.float32)
    query_sum, kv_full = lax.fori_loop(0, reach + 1, grads_step, (query_zero, kv_zero))
    kv_mine = lax.psum_scatter(kv_full, "ctx", scatter_dimension=1, tiled=True)
    grad_q = (query_sum * scale).reshape(rows, local_heads * group * head_size).astype(jnp.bfloat16)
    kv_b = kv_mine.astype(jnp.bfloat16)
    grad_k = kv_b[0].reshape(rows, local_heads * head_size)
    grad_v = kv_b[1].reshape(rows, local_heads * head_size)
    out_q, out_k, out_v = (
        lax.all_to_all(grad_q, "tp", split_axis=0, concat_axis=1, tiled=True),
        lax.all_to_all(grad_k, "tp", split_axis=0, concat_axis=1, tiled=True),
        lax.all_to_all(grad_v, "tp", split_axis=0, concat_axis=1, tiled=True),
    )
    return (out_q, out_k, out_v)


def solution(mesh):
    in_specs = (P("ctx", "tp"), P("ctx", "tp"), P("ctx", "tp"), P("ctx", "tp"), P())
    out_specs = (P(("ctx", "tp"), None), P(("ctx", "tp"), None), P(("ctx", "tp"), None))
    return jax.shard_map(local, mesh=mesh, in_specs=in_specs, out_specs=out_specs, check_vma=False)
```

profile of v0, /device:TPU:96, one launch (start us, length us, event | category | flops | bytes accessed | tf_op | source)
XLA Modules:
  0.0 493.7 jit_solution(12539389840710381137)
XLA Ops:
  7.2 1.5 pad_maximum_fusion
  9.7 1.1 copy.66
  11.0 1.1 copy.67
  13.0 86.4 %all-gather.2.cloned.1.call-done = bf16[2,8192,1,128]{3,1,2,0:T(8,128)(2,1)} async-done(((bf16[2,256,1,128]{3,1,2,0:T(8,128)(2,1)}), bf16[2,8192,1,128]{3,1,2,0:T(8,128)(2,1)}) %all-gather.2.cloned.1.call-update) | async-done | bytes 4194320 | tf_op jit(solution)/shard_map/all_gather | solution.py:109
  99.5 46.8 %while.38 = (s32[]{:T(128)}, f32[1,4,256]{2,1,0:T(4,128)S(1)}, f32[1,4,256]{2,1,0:T(4,128)S(1)}, f32[1,4,256]{2,1,0:T(4,128)S(1)}, s32[]{:T(128)}, /*index=5*/s3...) while((s32[]{:T(128)}, f32[1,4,256]{2,1,0:T(4,128)S(1)}, ...), condition=%wide.region_9.10_spmd.clone, body=%wide.region_2.9_spmd.clone.sunk | while | flops 137104912 | bytes 4142554 | solution.py:117
  100.9 2.8 conditional.6
  100.9 1.2 select_reduce_fusion
  102.2 1.3 fusion.6
  105.2 2.8 conditional.6
  105.2 1.2 select_reduce_fusion
  106.5 1.3 fusion.6
  109.5 2.8 conditional.6
  109.5 1.2 select_reduce_fusion
  110.8 1.3 fusion.6
  113.8 2.8 conditional.6
  113.8 1.2 select_reduce_fusion
  115.0 1.3 fusion.6
  118.1 2.8 conditional.6
  118.1 1.2 select_reduce_fusion
  119.3 1.3 fusion.6
  122.4 2.8 conditional.6
  122.4 1.2 select_reduce_fusion
  123.6 1.3 fusion.6
  126.6 2.8 conditional.6
  126.7 1.2 select_reduce_fusion
  127.9 1.3 fusion.6
  146.4 3.8 broadcast_in_dim.59
  150.1 86.6 %while.39 = (s32[]{:T(128)}, f32[256,1,4,128]{0,3,2,1:T(8,128)S(1)}, f32[2,8192,1,128]{3,1,2,0:T(8,128)}, s32[]{:T(128)}, s32[256]{0:T(256)S(1)}, /*index=5*/bf1...) while((s32[]{:T(128)}, ...), condition=%wide.region_14.15_spmd.clone, body=%wide.region_10.14_spmd.clone.sunk | while | flops 337936928 | bytes 9256414 | solution.py:129
  151.5 1.0 constant_dynamic-slice_fusion.2
  152.5 4.3 conditional.7
  152.5 1.3 fusion.17
  154.1 1.2 fusion.19
  155.3 1.2 fusion.20
  159.0 1.0 constant_dynamic-slice_fusion.2
  160.0 4.3 conditional.7
  160.0 1.3 fusion.17
  161.5 1.2 fusion.19
  162.7 1.2 fusion.20
  167.4 4.3 conditional.7
  167.4 1.3 fusion.17
  169.0 1.2 fusion.19
  170.2 1.2 fusion.20
  174.8 4.3 conditional.7
  174.9 1.3 fusion.17
  176.4 1.2 fusion.19
  177.6 1.2 fusion.20
  182.3 4.3 conditional.7
  182.3 1.3 fusion.17
  183.9 1.2 fusion.19
  185.1 1.2 fusion.20
  189.7 4.3 conditional.7
  189.7 1.3 fusion.17
  191.3 1.2 fusion.19
  192.5 1.2 fusion.20
  197.1 4.3 conditional.7
  197.1 1.3 fusion.17
  198.7 1.2 fusion.19
  199.9 1.2 fusion.20
  237.8 4.3 all-to-all-start
  242.1 222.3 %reduce-scatter.2.cloned.1.call-done = f32[2,256,1,128]{3,1,2,0:T(8,128)} async-done(((f32[2,8192,1,128]{3,1,2,0:T(8,128)}), f32[2,256,1,128]{3,1,2,0:T(8,128)}) %reduce-scatter.2.cloned.1.call-update) | async-done | bytes 262160 | tf_op jit(solution)/shard_map/reduce_scatter | solution.py:130
  466.0 4.3 all-to-all-start.1
  471.0 5.6 %all-to-all-done.1 = bf16[8,32,128]{2,1,0:T(8,128)(2,1)S(1)} async-done(((bf16[8,32,128]{2,1,0:T(8,128)(2,1)}), bf16[8,32,128]{2,1,0:T(8,128)(2,1)S(1)}, u32[]{:S(2)}, u32[]{:S(2)}) %all-to-all-start.1) | async-done | bytes 65568 | tf_op jit(solution)/shard_map/all_to_all | solution.py:137
  476.6 3.4 all-to-all-start.2
  480.6 5.6 %all-to-all-done.2 = bf16[8,32,128]{2,1,0:T(8,128)(2,1)S(1)} async-done(((bf16[8,32,128]{2,1,0:T(8,128)(2,1)}), bf16[8,32,128]{2,1,0:T(8,128)(2,1)S(1)}, u32[]{:S(2)}, u32[]{:S(2)}) %all-to-all-start.2) | async-done | bytes 65568 | tf_op jit(solution)/shard_map/all_to_all | solution.py:138
  (202 shorter events, 70.5 us)
Async XLA Ops:
  7.2 92.3 %all-gather.2.cloned.1.call-start = ((), (), s32[]{:S(2)}) async-start(), calls=%async_computation.4 | async-start | bytes 4325376 | tf_op jit(solution)/shard_map/all_gather | solution.py:109
  8.8 455.6 %reduce-scatter.2.cloned.1.call-start = ((), (), s32[]{:S(2)}) async-start(), calls=%async_computation.5 | async-start | bytes 8650752 | tf_op jit(solution)/shard_map/reduce_scatter | solution.py:130
  237.8 228.2 %all-to-all-start = ((bf16[8,32,512]{2,1,0:T(8,128)(2,1)}), bf16[8,32,512]{2,1,0:T(8,128)(2,1)S(1)}, u32[]{:S(2)}, u32[]{:S(2)}) async-start(bf16[8,32,512]{2,1,0:T(8,128)(2,1)} %convert_element_type.40), calls=%async_computation | async-start | bytes 524288 | tf_op jit(solution)/shard_map/all_to_all | solution.py:136
  466.0 10.6 %all-to-all-start.1 = ((bf16[8,32,128]{2,1,0:T(8,128)(2,1)}), bf16[8,32,128]{2,1,0:T(8,128)(2,1)S(1)}, u32[]{:S(2)}, u32[]{:S(2)}) async-start(bf16[8,32,128]{2,1,0:T(8,128)(2,1)} %bitcast.48), calls=%async_computation.2 | async-start | bytes 131072 | tf_op jit(solution)/shard_map/all_to_all | solution.py:137
  476.6 9.6 %all-to-all-start.2 = ((bf16[8,32,128]{2,1,0:T(8,128)(2,1)}), bf16[8,32,128]{2,1,0:T(8,128)(2,1)S(1)}, u32[]{:S(2)}, u32[]{:S(2)}) async-start(bf16[8,32,128]{2,1,0:T(8,128)(2,1)} %bitcast.50), calls=%async_computation.3 | async-start | bytes 131072 | tf_op jit(solution)/shard_map/all_to_all | solution.py:138
Sparse Core Ops, SparseCore 0:
  11.4 88.0 all-gather.1
  236.9 227.4 reduce-scatter.1
where the time goes:
time: 501 us; the launch traced here: 494 us
  waiting for transfers between devices  320 us (64%)
  matrix products  46.7 us (9%)
  local copies, waits for them, and re-layouts  41.2 us (8%)
  other arithmetic  34.2 us (7%)
  loops' own time  25.5 us (5%)
  between operations  14.1 us (3%)
  starting transfers between devices  12 us (2%)
    reduce_scatter x1, waiting for transfers between devices, local(): kv_mine = lax.psum_scatter(kv_full, 'ctx', scatter_dimension=1, tiled=True)  222 us
    all_gather x1, waiting for transfers between devices, local(): whole = lax.all_gather(kv_own, 'ctx', axis=1, tiled=True)  86.4 us
    and x36, other arithmetic, tile_mask(): (key_pos[None, :] >= starts[:, None]) & (key_pos[None, :] <= query_pos[:,...  28.6 us
    dynamic_slice x18, local copies, waits for them, and re-layouts, grads_step(): old = lax.dynamic_slice_in_dim(kv_full, first, rows, 1)  17.6 us
    dynamic_update_slice x18, local copies, waits for them, and re-layouts, grads_step(): return (query_sum, lax.dynamic_update_slice_in_dim(kv_full, new, first, 1))  12.9 us
    another operation x1, loops' own time, local(): stats = lax.fori_loop(0, reach + 1, stats_step, stats_init)  12.4 us
    another operation x1, loops' own time, local(): lax.fori_loop(0, reach + 1, grads_step, (query_zero, kv_zero))  12 us
  transfers between devices with their start and end apart: 5, of which 4 were waited for; matrix products, arithmetic and copies ran while one was open for 2% of the time, Pallas kernels for 0%

commit v1 on v0

v1 whole, which is shorter than its diff:
```python
import math

import jax
import jax.numpy as jnp
from jax import lax
from jax.experimental import pallas as pl
from jax.experimental.pallas import tpu as pltpu
from jax.sharding import Mesh, PartitionSpec as P

HD = 128
GROUP = 4
ROWS = 256
SLAB = 4
REACH = 5
HALF = 3
HERE = (0, 2)
THERE = (2, 4)
DOC_COUNT = 17
SCALE = HD ** -0.5
SCALE2 = SCALE * math.log2(math.e)
MASKED = -1e30
EMPTY = -1e29
VMEM_LIMIT = 16 * 1024 * 1024
NT = (((1,), (1,)), ((), ()))
NN = (((1,), (0,)), ((), ()))
F32 = jnp.float32
BF16 = jnp.bfloat16


def dot_nt(a, b):
    return lax.dot_general(a, b, NT, preferred_element_type=F32)


def dot_nn(a, b):
    return lax.dot_general(a, b, NN, preferred_element_type=F32)


def start_of(doc_ref, positions):
    end = jnp.int32(0)
    starts = jnp.zeros_like(positions)
    for doc in range(DOC_COUNT):
        length = doc_ref[doc]
        end = end + length
        starts = starts + jnp.where(end <= positions, length, 0)
    return starts


def tile_mask(doc_ref, query_block, key_block):
    positions = query_block * ROWS + lax.broadcasted_iota(jnp.int32, (1, ROWS), 1)
    starts = start_of(doc_ref, positions)
    key_pos = key_block * ROWS + lax.broadcasted_iota(jnp.int32, (ROWS, ROWS), 0)
    return (key_pos >= starts) & (key_pos <= positions)


def step_range(doc_ref, z, j, qb):
    first = start_of(doc_ref, (SLAB * z + qb) * ROWS) // ROWS
    low = jnp.maximum((first - j + SLAB - 1) >> 2, 0)
    return jnp.where(j <= qb, 0, 1), z - low


def pack_kernel(q_ref, g_ref, k_ref, v_ref, qg_ref, kv_ref, sems):
    wide, thin = GROUP * HD, HD
    copies = [
        pltpu.make_async_copy(k_ref, kv_ref.at[:, :thin], sems.at[0]),
        pltpu.make_async_copy(v_ref, kv_ref.at[:, thin:], sems.at[1]),
        pltpu.make_async_copy(q_ref, qg_ref.at[:, :wide], sems.at[2]),
        pltpu.make_async_copy(g_ref, qg_ref.at[:, wide:], sems.at[3]),
    ]
    for copy in copies:
        copy.start()
    for copy in copies:
        copy.wait()


def stats_steps(place_ref, doc_ref, rels, base, qg_all, kv_all, in_ref, out_ref):
    z, j = place_ref[0], place_ref[1]

    def per_block(rel, _):
        qb = j ^ rel
        low, high = step_range(doc_ref, z, j, qb)

        def per_step(k, carry):
            mask = tile_mask(doc_ref, SLAB * z + qb, SLAB * (z - k) + j)
            keys = kv_all[k, :, :HD]
            values = kv_all[k, :, HD:]
            new = []
            for h in range(GROUP):
                top, total, dot = carry[3 * h : 3 * h + 3]
                q = qg_all[rel, :, h * HD : (h + 1) * HD]
                g = qg_all[rel, :, (GROUP + h) * HD : (GROUP + h + 1) * HD]
                s = jnp.where(mask, dot_nt(keys, q) * SCALE2, MASKED)
                new_top = jnp.maximum(top, jnp.max(s, axis=0, keepdims=True))
                p = jnp.exp2(s - new_top)
                dp = dot_nt(values, g)
                factor = jnp.exp2(top - new_top)
                new += [
                    new_top,
                    total * factor + jnp.sum(p, axis=0, keepdims=True),
                    dot * factor + jnp.sum(p * dp, axis=0, keepdims=True),
                ]
            return tuple(new)

        if in_ref is None:
            zero = jnp.zeros((1, ROWS), F32)
            init = (jnp.full((1, ROWS), EMPTY, F32), zero, zero) * GROUP
        else:
            init = tuple(
                in_ref[part, pl.ds(qb * GROUP + h, 1), :]
                for h in range(GROUP)
                for part in range(3)
            )
        first, end = jnp.maximum(low, base), jnp.minimum(high + 1, base + HALF)
        done = lax.fori_loop(first, end, per_step, init)
        for h in range(GROUP):
            for part in range(3):
                out_ref[part, pl.ds(qb * GROUP + h, 1), :] = done[3 * h + part]
        return 0

    lax.fori_loop(rels[0], rels[1], per_block, 0)


def here_stats_kernel(place_ref, doc_ref, qg0, qg1, kv0, kv1, kv2, out_ref, kv_near, qg_here):
    for slot, ref in enumerate((qg0, qg1)):
        qg_here[slot] = ref[...]
    for slot, ref in enumerate((kv0, kv1, kv2)):
        kv_near[slot] = ref[...]
    stats_steps(place_ref, doc_ref, HERE, 0, qg_here, kv_near, None, out_ref)


def there_stats_kernel(place_ref, doc_ref, in_ref, kv_near, qg0, qg1, qg2, qg3, out_ref, qg_all):
    for slot, ref in enumerate((qg0, qg1, qg2, qg3)):
        qg_all[slot] = ref[...]
    out_ref[...] = in_ref[...]
    stats_steps(place_ref, doc_ref, THERE, 0, qg_all, kv_near, None, out_ref)


def far_stats_kernel(place_ref, doc_ref, in_ref, qg_all, kv_near, kv3, kv4, kv5, out_ref, kv_all):
    kv_all[:HALF] = kv_near[...]
    for slot, ref in enumerate((kv3, kv4, kv5)):
        kv_all[HALF + slot] = ref[...]
    stats_steps(place_ref, doc_ref, (0, SLAB), HALF, qg_all, kv_all, in_ref, out_ref)


def combine_stats(st_refs, lse_buf, delta_buf):
    stats = [ref[...] for ref in st_refs]
    top = jnp.maximum(
        jnp.maximum(stats[0][0], stats[1][0]), jnp.maximum(stats[2][0], stats[3][0])
    )
    total = jnp.zeros_like(top)
    dot = jnp.zeros_like(top)
    for st in stats:
        factor = jnp.exp2(st[0] - top)
        total = total + st[1] * factor
        dot = dot + st[2] * factor
    lse_buf[...] = top + jnp.log2(total)
    delta_buf[...] = dot / total


def visit_step(
    place_ref, doc_ref, k, rels, first, qg_all, kv_all, lse_buf, delta_buf, dqt, acc
):
    z, j = place_ref[0], place_ref[1]
    keys_t = kv_all[k, :, :HD].astype(F32).T.astype(BF16)

    def per_block(rel, _):
        qb = j ^ rel
        low, high = step_range(doc_ref, z, j, qb)

        @pl.when((k >= low) & (k <= high))
        def _():
            mask = tile_mask(doc_ref, SLAB * z + qb, SLAB * (z - k) + j)
            keys = kv_all[k, :, :HD]
            values = kv_all[k, :, HD:]
            dk = dv = None
            for h in range(GROUP):
                q = qg_all[rel, :, h * HD : (h + 1) * HD]
                g = qg_all[rel, :, (GROUP + h) * HD : (GROUP + h + 1) * HD]
                lse = lse_buf[pl.ds(qb * GROUP + h, 1), :]
                delta = delta_buf[pl.ds(qb * GROUP + h, 1), :]
                p = jnp.where(mask, jnp.exp2(dot_nt(keys, q) * SCALE2 - lse), 0.0)
                ds = p * (dot_nt(values, g) - delta)
                pb = p.astype(BF16)
                dsb = ds.astype(BF16)
                dv_add, dk_add = dot_nn(pb, g), dot_nn(dsb, q)
                dv = dv_add if dv is None else dv + dv_add
                dk = dk_add if dk is None else dk + dk_add
                dqt[(rel - first) * GROUP + h] += dot_nn(keys_t, dsb)
            acc[:, :HD] += dk
            acc[:, HD:] += dv

        return 0

    lax.fori_loop(rels[0], rels[1], per_block, 0)


def write_dq(dqt, slot, out_ref):
    for h in range(GROUP):
        dq = dqt[slot * GROUP + h].T * SCALE
        out_ref[:, h * HD : (h + 1) * HD] = dq.astype(BF16)


def write_dkv(out_ref, slot, acc):
    out_ref[slot, :, :HD] = (acc[:, :HD] * SCALE).astype(out_ref.dtype)
    out_ref[slot, :, HD:] = acc[:, HD:].astype(out_ref.dtype)


def far_kernel(
    place_ref, doc_ref, st0, st1, st2, st3, qg_all, kv_all,
    dqt_ref, dkv_ref, acc0_ref, lse_ref, delta_ref, acc,
):
    combine_stats((st0, st1, st2, st3), lse_ref, delta_ref)
    dqt_ref[...] = jnp.zeros_like(dqt_ref)

    def per_step(step, _):
        k = jnp.where(step == 0, 0, REACH + 1 - step)
        acc[...] = jnp.zeros_like(acc)
        visit_step(
            place_ref, doc_ref, k, (jnp.where(step == 0, THERE[0], 0), SLAB), 0,
            qg_all, kv_all, lse_ref, delta_ref, dqt_ref, acc,
        )

        @pl.when(step == 0)
        def _():
            acc0_ref[...] = acc[...]

        @pl.when(step > 0)
        def _():
            write_dkv(dkv_ref, k - HALF, acc)

        return 0

    lax.fori_loop(0, HALF + 1, per_step, 0)


def near_kernel(
    place_ref, doc_ref, lse_ref, delta_ref, qg_all, kv_all, dqt_in,
    dqt_out, keep_ref, send_ref, dkv_ref, dqt, acc,
):
    dqt[...] = dqt_in[...]

    def per_step(step, _):
        k = 2 - step
        acc[...] = jnp.zeros_like(acc)
        visit_step(
            place_ref, doc_ref, k, (0, SLAB), 0,
            qg_all, kv_all, lse_ref, delta_ref, dqt, acc,
        )
        write_dkv(dkv_ref, k - 1, acc)
        return 0

    lax.fori_loop(0, 2, per_step, 0)
    write_dq(dqt, 2, keep_ref)
    write_dq(dqt, 3, send_ref)
    dqt_out[...] = dqt[: 2 * GROUP]


def own_kernel(
    place_ref, doc_ref, lse_ref, delta_ref, qg_all, kv_all, dqt_in, acc0,
    keep_ref, send_ref, dkv_ref, dqt, acc,
):
    dqt[...] = dqt_in[...]
    acc[...] = acc0[...]
    visit_step(
        place_ref, doc_ref, jnp.int32(0), HERE, 0,
        qg_all, kv_all, lse_ref, delta_ref, dqt, acc,
    )
    write_dkv(dkv_ref, 0, acc)
    write_dq(dqt, 0, keep_ref)
    write_dq(dqt, 1, send_ref)


def pair_kernel(keep, got, out_ref):
    out_ref[...] = (keep[...].astype(F32) + got[...].astype(F32)).astype(BF16)


def merge_kernel(keep, beside, across, dkv0, got1, got2, got5, out_ref):
    parts, part = out_ref.shape[:2]
    width = GROUP * HD
    dq = keep[...].astype(F32) + beside[...].astype(F32) + across[...].astype(F32)
    dkv = dkv0[0] + got1[...].astype(F32) + got2[...].astype(F32) + got5[...].astype(F32)
    out_ref[:, :, :width] = dq.astype(BF16).reshape(parts, part, width)
    out_ref[:, :, width:] = dkv.astype(BF16).reshape(parts, part, 2 * HD)


def finish_kernel(got, q_ref, k_ref, v_ref):
    width = GROUP * HD
    for t in range(got.shape[0]):
        q_ref[:, t * width : (t + 1) * width] = got[t, :, :width]
        k_ref[:, t * HD : (t + 1) * HD] = got[t, :, width : width + HD]
        v_ref[:, t * HD : (t + 1) * HD] = got[t, :, width + HD :]


SMEM_SPEC = pl.BlockSpec(memory_space=pltpu.SMEM)
VMEM_SPEC = pl.BlockSpec(memory_space=pltpu.VMEM)


def call(kernel, name, outs, scratch, *args, scalars=2):
    return pl.pallas_call(
        kernel,
        out_shape=tuple(jax.ShapeDtypeStruct(shape, dtype) for shape, dtype in outs),
        in_specs=[SMEM_SPEC] * scalars + [VMEM_SPEC] * (len(args) - scalars),
        out_specs=(VMEM_SPEC,) * len(outs),
        scratch_shapes=[pltpu.VMEM(shape, dtype) for shape, dtype in scratch],
        compiler_params=pltpu.CompilerParams(vmem_limit_bytes=VMEM_LIMIT),
        cost_estimate=pl.CostEstimate(flops=1, bytes_accessed=1, transcendentals=0),
        name=name,
    )(*args)


QG_ALL = ((SLAB, ROWS, 2 * GROUP * HD), BF16)
QG_HERE = ((2, ROWS, 2 * GROUP * HD), BF16)
KV_ALL = ((REACH + 1, ROWS, 2 * HD), BF16)
KV_NEAR = ((HALF, ROWS, 2 * HD), BF16)
STATS = ((3, SLAB * GROUP, ROWS), F32)
ROW_STATS = ((SLAB * GROUP, ROWS), F32)
DQT = ((SLAB * GROUP, HD, ROWS), F32)
DQT_HALF = ((2 * GROUP, HD, ROWS), F32)
ACC = ((ROWS, 2 * HD), F32)
DQ = ((ROWS, GROUP * HD), BF16)


def flip(x, axis):
    return lax.ppermute(x, axis, [(0, 1), (1, 0)])


def shift(x, by, slabs):
    pairs = [(i, i + by) for i in range(slabs) if 0 <= i + by < slabs]
    return lax.ppermute(x, "z", pairs)


def shift_last(x, by, slabs):
    last = SLAB - 1
    pairs = [
        (i * SLAB + last, (i + by) * SLAB + last) for i in range(slabs) if 0 <= i + by < slabs
    ]
    return lax.ppermute(x, ("z", "y", "core"), pairs)


def local(queries, keys, values, grad_out, doc_lengths):
    z = lax.axis_index("z")
    j = lax.axis_index(("y", "core"))
    slabs = lax.axis_size("z")
    place = jnp.stack((z, j)).astype(jnp.int32)

    qg, kv = pl.pallas_call(
        pack_kernel,
        out_shape=(
            jax.ShapeDtypeStruct((ROWS, 2 * GROUP * HD), BF16),
            jax.ShapeDtypeStruct((ROWS, 2 * HD), BF16),
        ),
        in_specs=[pl.BlockSpec(memory_space=pltpu.HBM)] * 4,
        out_specs=(VMEM_SPEC,) * 2,
        scratch_shapes=[pltpu.SemaphoreType.DMA((4,))],
        compiler_params=pltpu.CompilerParams(vmem_limit_bytes=56 * 1024 * 1024),
        cost_estimate=pl.CostEstimate(flops=1, bytes_accessed=1, transcendentals=0),
        name="pack",
    )(queries, grad_out, keys, values)
    across = flip(qg, "y")
    kv1 = shift(kv, 1, slabs)
    kv2 = shift(kv, 2, slabs)
    beside = flip(qg, "core")
    kv5 = shift_last(kv, 5, slabs)
    kv2 = lax.optimization_barrier(kv2)
    kv3 = shift(kv2, 1, slabs)

    stats, kv_near = call(
        here_stats_kernel, "here_statistics", [STATS, KV_NEAR], [QG_HERE],
        place, doc_lengths, qg, beside, kv, kv1, kv2,
    )
    across, stats, kv3, kv5 = lax.optimization_barrier((across, stats, kv3, kv5))
    kv4 = shift(kv3, 1, slabs)
    both = flip(across, "core")
    stats, qg_all = call(
        there_stats_kernel, "there_statistics", [STATS, QG_ALL], [],
        place, doc_lengths, stats, kv_near, qg, beside, across, both,
    )
    stats, kv_all = call(
        far_stats_kernel, "far_statistics", [STATS, KV_ALL], [],
        place, doc_lengths, stats, qg_all, kv_near, kv3, kv4, kv5,
    )
    stats_y = flip(stats, "y")
    stats_c = flip(stats, "core")
    stats_yc = flip(stats_y, "core")

    dqt, dkv_far, acc0, lse, delta = call(
        far_kernel, "far_gradients",
        [DQT, ((HALF,) + ACC[0], BF16), ACC, ROW_STATS, ROW_STATS], [ACC],
        place, doc_lengths, stats, stats_c, stats_y, stats_yc, qg_all, kv_all,
    )
    got_far = shift(dkv_far[:2], -2, slabs)
    got5 = shift_last(dkv_far[2], -5, slabs)
    dqt, there_keep, there_send, dkv_near = call(
        near_kernel, "near_gradients",
        [DQT_HALF, DQ, DQ, ((2,) + ACC[0], F32)], [DQT, ACC],
        place, doc_lengths, lse, delta, qg_all, kv_all, dqt,
    )
    there_got = flip(there_send, "core")
    dkv_send = (dkv_near + got_far.astype(F32)).astype(BF16)
    dq_pair, = call(pair_kernel, "pair", [DQ], [], there_keep, there_got, scalars=0)
    dkv_send, dq_pair, dqt = lax.optimization_barrier((dkv_send, dq_pair, dqt))
    got2 = shift(dkv_send[1], -2, slabs)
    got1 = shift(dkv_send[0], -1, slabs)
    dq_across = flip(dq_pair, "y")
    dq_keep, dq_send, dkv0 = call(
        own_kernel, "own_gradients",
        [DQ, DQ, ((1,) + ACC[0], F32)], [DQT_HALF, ACC],
        place, doc_lengths, lse, delta, qg_all, kv_all, dqt, acc0,
    )
    dq_send, dq_across, got1, got2, got5 = lax.optimization_barrier(
        (dq_send, dq_across, got1, got2, got5)
    )
    dq_beside = flip(dq_send, "core")

    tp = lax.axis_size("tp")
    part = ROWS // tp
    width = GROUP * HD
    whole, = call(
        merge_kernel, "merge", [((tp, part, width + 2 * HD), BF16)], [],
        dq_keep, dq_beside, dq_across, dkv0, got1, got2, got5, scalars=0,
    )
    got = lax.all_to_all(whole, "tp", split_axis=0, concat_axis=0, tiled=True)
    return call(
        finish_kernel, "finish",
        [((part, tp * width), BF16), ((part, tp * HD), BF16), ((part, tp * HD), BF16)], [],
        got, scalars=0,
    )


def solution(mesh):
    tp = mesh.shape["tp"]
    inner = Mesh(mesh.devices.reshape(-1, 2, 2, tp), ("z", "y", "core", "tp"))
    tokens = ("z", "y", "core")
    in_specs = (P(tokens, "tp"),) * 4 + (P(),)
    out_specs = (P(tokens + ("tp",), None),) * 3
    return jax.shard_map(local, mesh=inner, in_specs=in_specs, out_specs=out_specs, check_vma=False)
```

time: 501 us -> 99.6 us (0.20); the launches traced: 494 us -> 99.2 us
  waiting for transfers between devices: 320 us -> 27.2 us
  matrix products: 46.7 us -> 0 us
  local copies, waits for them, and re-layouts: 41.2 us -> 2.65 us
  other arithmetic: 34.2 us -> 0.13 us
  loops' own time: 25.5 us -> 0 us
  starting transfers between devices: 12 us -> 37.3 us
  Pallas kernels: 0 us -> 16.9 us
  blocking collectives: 0 us -> 14.1 us
  between operations: 14.1 us -> 0.89 us
    reduce_scatter x1 -> x0, waiting for transfers between devices: 222 us -> none  [local(): kv_mine = lax.psum_scatter(kv_full, 'ctx', scatter_dimension=1, tiled=True)]
    all_gather x1 -> x0, waiting for transfers between devices: 86.4 us -> none  [local(): whole = lax.all_gather(kv_own, 'ctx', axis=1, tiled=True)]
    dot_general x49 -> x0, matrix products: 46.7 us -> none  [the longest x7 8.87 us: grad_core(): jnp.einsum('qhgd,khd->hgqk', query_heads, block[0], preferred_element_typ...]
    ppermute x0 -> x18, starting transfers between devices: none -> 37.3 us  [the longest x7 26.8 us: shift(): return lax.ppermute(x, 'z', pairs)]
    and x36 -> x0, other arithmetic: 28.6 us -> none  [tile_mask(): (key_pos[None, :] >= starts[:, None]) & (key_pos[None, :] <= query_pos[:,...]
    ppermute x0 -> x18, waiting for transfers between devices: none -> 27.2 us  [the longest x7 20.4 us: shift(): return lax.ppermute(x, 'z', pairs)]
    another operation x38 -> x0, loops' own time: 25.5 us -> none  [the longest x1 12.4 us: local(): stats = lax.fori_loop(0, reach + 1, stats_step, stats_init)]
    dynamic_slice x18 -> x0, local copies, waits for them, and re-layouts: 17.6 us -> none  [grads_step(): old = lax.dynamic_slice_in_dim(kv_full, first, rows, 1)]
  transfers between devices with their start and end apart: 5 -> 18, of which waited for: 4 -> 8; matrix products, arithmetic and copies ran while one was open for 2% -> 0% of each run, Pallas kernels for 0% -> 9%
where the time goes in v1:
time: 99.6 us; the launch traced here: 99.2 us
  starting transfers between devices  37.3 us (37%)
  waiting for transfers between devices  27.2 us (27%)
  Pallas kernels  16.9 us (17%)
  blocking collectives  14.1 us (14%)
  local copies, waits for them, and re-layouts  2.65 us (3%)
    ppermute x7, starting transfers between devices, shift(): return lax.ppermute(x, 'z', pairs)  26.8 us
    ppermute x7, waiting for transfers between devices, shift(): return lax.ppermute(x, 'z', pairs)  20.4 us
    pallas_call x9, Pallas kernels, call(): pl.pallas_call(kernel, out_shape=tuple((jax.ShapeDtypeStruct(shape, dtype...  15 us
    all_to_all x1, blocking collectives, local(): got = lax.all_to_all(whole, 'tp', split_axis=0, concat_axis=0, tiled=True)  14.1 us
    ppermute x9, starting transfers between devices, flip(): return lax.ppermute(x, axis, [(0, 1), (1, 0)])  9.22 us
    ppermute x9, waiting for transfers between devices, flip(): return lax.ppermute(x, axis, [(0, 1), (1, 0)])  6.79 us
    unnamed x8, local copies, waits for them, and re-layouts  2.61 us
  transfers between devices with their start and end apart: 18, of which 8 were waited for; matrix products, arithmetic and copies ran while one was open for 0% of the time, Pallas kernels for 9%

profile of v1, /device:TPU:96, one launch (start us, length us, event | category | flops | bytes accessed | tf_op | source)
XLA Modules:
  0.0 99.2 jit_solution(2585035001057644486)
XLA Ops:
  0.6 0.0 copy-start.3
  0.6 2.0 %pack.1 = (bf16[256,1024]{1,0:T(8,128)(2,1)}, bf16[256,256]{1,0:T(8,128)(2,1)}) custom-call(bf16[256,512]{1,0:T(8,128)(2,1)} %q_ref.1, bf16[256,512]{1,0:T(8,128)(2,1)} %g_ref.1, bf16[256,128]{1,0:T(8,128)(2,1)} %k_ref.1, bf16[256,128]{1,0:T(8,128)(2,1)} %v_ref.1), custom_call_target="tpu_custom_call" | custom-call | flops 1 | bytes 1 | tf_op jit(solution)/shard_map/pack/pallas_call | solution.py:345
  2.6 0.1 collective-permute-start.1
  2.7 3.3 %collective-permute-start = (bf16[256,1024]{1,0:T(8,128)(2,1)}, bf16[256,1024]{1,0:T(8,128)(2,1)S(1)}, u32[]{:S(2)}, u32[]{:S(2)}) collective-permute-start(bf16[256,1024]{1,0:T(8,128)(2,1)} %get-tuple-element.35.qg0), channel_id=1, source_target_pairs={{0,16},{16,0},{1,17},{17,1},{2,18},{18,2},{3,19},{19,3},{4,20},{20... | collective-permute-start | bytes 1572872 | tf_op jit(solution)/shard_map/ppermute | solution.py:323
  6.0 5.5 %collective-permute-start.3 = (bf16[256,256]{1,0:T(8,128)(2,1)}, bf16[256,256]{1,0:T(8,128)(2,1)S(1)}, u32[]{:S(2)}, u32[]{:S(2)}) collective-permute-start(bf16[256,256]{1,0:T(8,128)(2,1)} %get-tuple-element.36.kv0), channel_id=1, source_target_pairs={{0,64},{32,96},{64,128},{96,160},{128,192},{160,224},{1,65},{33,97... | collective-permute-start | bytes 393224 | tf_op jit(solution)/shard_map/ppermute | solution.py:328
  11.5 2.9 %collective-permute-start.2 = (bf16[256,256]{1,0:T(8,128)(2,1)}, bf16[256,256]{1,0:T(8,128)(2,1)S(1)}, u32[]{:S(2)}, u32[]{:S(2)}) collective-permute-start(bf16[256,256]{1,0:T(8,128)(2,1)} %get-tuple-element.36.kv0), channel_id=1, source_target_pairs={{0,32},{32,64},{64,96},{96,128},{128,160},{160,192},{192,224},{1,3... | collective-permute-start | bytes 393224 | tf_op jit(solution)/shard_map/ppermute | solution.py:328
  14.4 0.7 collective-permute-start.5
  15.1 1.9 %collective-permute-done.3.kv2 = bf16[256,256]{1,0:T(8,128)(2,1)S(1)} collective-permute-done((bf16[256,256]{1,0:T(8,128)(2,1)}, bf16[256,256]{1,0:T(8,128)(2,1)S(1)}, u32[]{:S(2)}, u32[]{:S(2)}) %collective-permute-start.3) | collective-permute-done | bytes 131104 | tf_op jit(solution)/shard_map/ppermute | solution.py:328
  17.0 7.3 %collective-permute-start.4 = (bf16[256,256]{1,0:T(8,128)(2,1)S(1)}, bf16[256,256]{1,0:T(8,128)(2,1)S(1)}, u32[]{:S(2)}, u32[]{:S(2)}) collective-permute-start(bf16[256,256]{1,0:T(8,128)(2,1)S(1)} %collective-permute-done.3.kv2), channel_id=1, source_target_pairs={{0,32},{32,64},{64,96},{96,128},{128,160},{160,192},{192,224},{1,3... | collective-permute-start | bytes 393224 | tf_op jit(solution)/shard_map/ppermute | solution.py:328
  24.3 0.1 pad_add_fusion.place_ref
  24.4 0.0 collective-permute-done.2.kv1
  24.4 0.0 collective-permute-done.1.qg1
  24.4 0.0 copy-start
  24.4 1.0 %copy-done = bf16[256,1024]{1,0:T(8,128)(2,1)S(1)} copy-done((bf16[256,1024]{1,0:T(8,128)(2,1)S(1)}, bf16[256,1024]{1,0:T(8,128)(2,1)}, u32[]{:S(2)}) %copy-start) | copy-done | bytes 524312
  25.5 0.0 copy-start.1
  25.5 0.9 copy-done.1
  26.4 0.0 copy-start.2
  26.4 0.7 copy-done.2
  27.0 1.9 %here_statistics.1 = (f32[3,16,256]{2,1,0:T(8,128)S(1)}, bf16[3,256,256]{2,1,0:T(8,128)(2,1)S(1)}) custom-call(s32[2]{0:T(128)S(1)} %pad_add_fusion.place_ref, s32[17]{0:T(128)S(1)} %copy-done.2, bf16[256,1024]{1,0:T(8,128)(2,1)S(1)} %copy-done, bf16[256,1024]{1,0:T(8,128)(2,1)S(1)} %collective-permute-done.1.qg1, bf16[256,256]{1,0:T(8,128)(2,1)S(1)} %copy-done.1, ...), custom_call_target="tpu_custom_call" | custom-call | flops 1 | bytes 1 | tf_op jit(solution)/shard_map/here_statistics/pallas_call | solution.py:298
  29.0 0.0 collective-permute-done.5.kv5
  29.0 0.0 collective-permute-done.4.kv3
  29.0 0.0 collective-permute-done.qg2
  29.0 0.1 collective-permute-start.6
  29.1 3.3 %collective-permute-start.7 = (bf16[256,256]{1,0:T(8,128)(2,1)S(1)}, bf16[256,256]{1,0:T(8,128)(2,1)S(1)}, u32[]{:S(2)}, u32[]{:S(2)}) collective-permute-start(bf16[256,256]{1,0:T(8,128)(2,1)S(1)} %collective-permute-done.4.kv3), channel_id=1, source_target_pairs={{0,32},{32,64},{64,96},{96,128},{128,160},{160,192},{192,224},{1,3... | collective-permute-start | bytes 393224 | tf_op jit(solution)/shard_map/ppermute | solution.py:328
  32.4 0.0 collective-permute-done.6.qg3
  32.4 0.0 copy-done.3
  32.4 2.0 %there_statistics.1 = (f32[3,16,256]{2,1,0:T(8,128)S(1)}, bf16[4,256,1024]{2,1,0:T(8,128)(2,1)S(1)}) custom-call(s32[2]{0:T(128)S(1)} %pad_add_fusion.place_ref, s32[17]{0:T(128)S(1)} %copy-done.3, f32[3,16,256]{2,1,0:T(8,128)S(1)} %get-tuple-element.38.in_ref, bf16[3,256,256]{2,1,0:T(8,128)(2,1)S(1)} %get-tuple-element.39.kv_near, ...), custom_call_target="tpu_custom_call" | custom-call | flops 1 | bytes 1 | tf_op jit(solution)/shard_map/there_statistics/pallas_call | solution.py:298
  34.4 2.5 %collective-permute-done.7.kv4 = bf16[256,256]{1,0:T(8,128)(2,1)S(1)} collective-permute-done((bf16[256,256]{1,0:T(8,128)(2,1)S(1)}, bf16[256,256]{1,0:T(8,128)(2,1)S(1)}, u32[]{:S(2)}, u32[]{:S(2)}) %collective-permute-start.7) | collective-permute-done | bytes 131104 | tf_op jit(solution)/shard_map/ppermute | solution.py:328
  36.9 0.8 far_statistics.1
  37.7 1.6 %collective-permute-start.9 = (f32[3,16,256]{2,1,0:T(8,128)S(1)}, f32[3,16,256]{2,1,0:T(8,128)S(1)}, u32[]{:S(2)}, u32[]{:S(2)}) collective-permute-start(f32[3,16,256]{2,1,0:T(8,128)S(1)} %get-tuple-element.45.st0), channel_id=1, source_target_pairs={{0,16},{16,0},{1,17},{17,1},{2,18},{18,2},{3,19},{19,3},{4,20},{20... | collective-permute-start | bytes 147464 | tf_op jit(solution)/shard_map/ppermute | solution.py:323
  39.3 0.0 collective-permute-start.8
  39.3 4.0 %collective-permute-done.9.st2 = f32[3,16,256]{2,1,0:T(8,128)S(1)} collective-permute-done((f32[3,16,256]{2,1,0:T(8,128)S(1)}, f32[3,16,256]{2,1,0:T(8,128)S(1)}, u32[]{:S(2)}, u32[]{:S(2)}) %collective-permute-start.9) | collective-permute-done | bytes 49184 | tf_op jit(solution)/shard_map/ppermute | solution.py:323
  43.4 0.0 collective-permute-start.10
  43.4 0.0 collective-permute-done.8.st1
  43.4 1.2 %collective-permute-done.10.st3 = f32[3,16,256]{2,1,0:T(8,128)S(1)} collective-permute-done((f32[3,16,256]{2,1,0:T(8,128)S(1)}, f32[3,16,256]{2,1,0:T(8,128)S(1)}, u32[]{:S(2)}, u32[]{:S(2)}) %collective-permute-start.10) | collective-permute-done | bytes 49184 | tf_op jit(solution)/shard_map/ppermute | solution.py:323
  44.6 4.2 %far_gradients.1 = (f32[16,128,256]{2,1,0:T(8,128)S(1)}, bf16[3,256,256]{2,1,0:T(8,128)(2,1)S(1)}, f32[256,256]{1,0:T(8,128)S(1)}, f32[16,256]{1,0:T(8,128)S(1)}, f32[16,256]{1,0:T(8,128)S(1)}) custom-call(s32[2]{0:T(128)S(1)} %pad_add_fusion.place_ref, s32[17]{0:T(128)S(1)} %copy-done.3, f32[3,16,256]{2,1,0:T(8,128)S(1)} %get-tuple-element.45.st0, ...), custom_call_target="tpu_custom_call" | custom-call | flops 1 | bytes 1 | tf_op jit(solution)/shard_map/far_gradients/pallas_call | solution.py:298
  48.8 1.9 %collective-permute-start.11 = (bf16[2,256,256]{2,1,0:T(8,128)(2,1)S(1)}, bf16[2,256,256]{2,1,0:T(8,128)(2,1)S(1)}, u32[]{:S(2)}, u32[]{:S(2)}) collective-permute-start(bf16[2,256,256]{2,1,0:T(8,128)(2,1)S(1)} %slice.12), channel_id=1, source_target_pairs={{64,0},{96,32},{128,64},{160,96},{192,128},{224,160},{65,1},{97,33... | collective-permute-start | bytes 786440 | tf_op jit(solution)/shard_map/ppermute | solution.py:328
  50.8 1.6 %near_gradients.1 = (f32[8,128,256]{2,1,0:T(8,128)S(1)}, bf16[256,512]{1,0:T(8,128)(2,1)S(1)}, bf16[256,512]{1,0:T(8,128)(2,1)S(1)}, f32[2,256,256]{2,1,0:T(8,128)S(1)}) custom-call(s32[2]{0:T(128)S(1)} %pad_add_fusion.place_ref, s32[17]{0:T(128)S(1)} %copy-done.3, f32[16,256]{1,0:T(8,128)S(1)} %get-tuple-element.47.lse_ref, ...), custom_call_target="tpu_custom_call" | custom-call | flops 1 | bytes 1 | tf_op jit(solution)/shard_map/near_gradients/pallas_call | solution.py:298
  52.4 0.2 collective-permute-start.12
  52.6 0.7 collective-permute-start.16
  53.3 8.0 %collective-permute-done.11 = bf16[2,256,256]{2,1,0:T(8,128)(2,1)S(1)} collective-permute-done((bf16[2,256,256]{2,1,0:T(8,128)(2,1)S(1)}, bf16[2,256,256]{2,1,0:T(8,128)(2,1)S(1)}, u32[]{:S(2)}, u32[]{:S(2)}) %collective-permute-start.11) | collective-permute-done | bytes 262176 | tf_op jit(solution)/shard_map/ppermute | solution.py:328
  61.3 0.1 add_convert_fusion
  61.4 0.0 collective-permute-done.12.got
  61.4 0.1 pair.1
  61.4 3.9 %collective-permute-start.13 = (bf16[256,512]{1,0:T(8,128)(2,1)S(1)}, bf16[256,512]{1,0:T(8,128)(2,1)S(1)}, u32[]{:S(2)}, u32[]{:S(2)}) collective-permute-start(bf16[256,512]{1,0:T(8,128)(2,1)S(1)} %pair.1), channel_id=1, source_target_pairs={{0,16},{16,0},{1,17},{17,1},{2,18},{18,2},{3,19},{19,3},{4,20},{20... | collective-permute-start | bytes 786440 | tf_op jit(solution)/shard_map/ppermute | solution.py:323
  65.3 2.0 %collective-permute-start.15 = (bf16[256,256]{1,0:T(8,128)(2,1)S(1)}, bf16[256,256]{1,0:T(8,128)(2,1)S(1)}, u32[]{:S(2)}, u32[]{:S(2)}) collective-permute-start(bf16[256,256]{1,0:T(8,128)(2,1)S(1)} %get-tuple-element.67), channel_id=1, source_target_pairs={{64,0},{96,32},{128,64},{160,96},{192,128},{224,160},{65,1},{97,33... | collective-permute-start | bytes 393224 | tf_op jit(solution)/shard_map/ppermute | solution.py:328
  67.3 3.9 %collective-permute-start.14 = (bf16[256,256]{1,0:T(8,128)(2,1)S(1)}, bf16[256,256]{1,0:T(8,128)(2,1)S(1)}, u32[]{:S(2)}, u32[]{:S(2)}) collective-permute-start(bf16[256,256]{1,0:T(8,128)(2,1)S(1)} %get-tuple-element.68), channel_id=1, source_target_pairs={{32,0},{64,32},{96,64},{128,96},{160,128},{192,160},{224,192},{33,... | collective-permute-start | bytes 393224 | tf_op jit(solution)/shard_map/ppermute | solution.py:328
  71.2 3.4 %own_gradients.1 = (bf16[256,512]{1,0:T(8,128)(2,1)S(1)}, bf16[256,512]{1,0:T(8,128)(2,1)S(1)}, f32[1,256,256]{2,1,0:T(8,128)S(1)}) custom-call(s32[2]{0:T(128)S(1)} %pad_add_fusion.place_ref, s32[17]{0:T(128)S(1)} %copy-done.3, f32[16,256]{1,0:T(8,128)S(1)} %get-tuple-element.47.lse_ref, f32[16,256]{1,0:T(8,128)S(1)} %get-tuple-element.48.delta_ref, ...), custom_call_target="tpu_custom_call" | custom-call | flops 1 | bytes 1 | tf_op jit(solution)/shard_map/own_gradients/pallas_call | solution.py:298
  74.6 0.0 collective-permute-done.16.got5
  74.6 2.5 %collective-permute-done.15.got2 = bf16[256,256]{1,0:T(8,128)(2,1)S(1)} collective-permute-done((bf16[256,256]{1,0:T(8,128)(2,1)S(1)}, bf16[256,256]{1,0:T(8,128)(2,1)S(1)}, u32[]{:S(2)}, u32[]{:S(2)}) %collective-permute-start.15) | collective-permute-done | bytes 131104 | tf_op jit(solution)/shard_map/ppermute | solution.py:328
  77.1 5.5 %collective-permute-done.14.got1 = bf16[256,256]{1,0:T(8,128)(2,1)S(1)} collective-permute-done((bf16[256,256]{1,0:T(8,128)(2,1)S(1)}, bf16[256,256]{1,0:T(8,128)(2,1)S(1)}, u32[]{:S(2)}, u32[]{:S(2)}) %collective-permute-start.14) | collective-permute-done | bytes 131104 | tf_op jit(solution)/shard_map/ppermute | solution.py:328
  82.6 0.0 collective-permute-done.13.across
  82.6 0.0 collective-permute-start.17
  82.7 1.5 %collective-permute-done.17.beside = bf16[256,512]{1,0:T(8,128)(2,1)S(1)} collective-permute-done((bf16[256,512]{1,0:T(8,128)(2,1)S(1)}, bf16[256,512]{1,0:T(8,128)(2,1)S(1)}, u32[]{:S(2)}, u32[]{:S(2)}) %collective-permute-start.17) | collective-permute-done | bytes 262176 | tf_op jit(solution)/shard_map/ppermute | solution.py:323
  84.2 0.2 merge.1
  84.3 14.1 %all_to_all.5.got = bf16[8,32,768]{2,1,0:T(8,128)(2,1)S(1)} all-to-all(bf16[8,32,768]{2,1,0:T(8,128)(2,1)S(1)} %merge.1), channel_id=1, replica_groups=mesh['z'=8,'y'=2,'core'=2,'tp'=8] {'tp'}, dimensions={0} | all-to-all | bytes 786432 | tf_op jit(solution)/shard_map/all_to_all | solution.py:421
  98.4 0.8 finish.1
  (3 shorter events, 0.0 us)
Async XLA Ops:
  0.6 31.8 %copy-start.3 = (s32[17]{0:T(128)S(1)}, s32[17]{0:T(128)}, u32[]{:S(2)}) copy-start(s32[17]{0:T(128)} %doc_ref.11) | copy-start | bytes 208
  2.6 21.8 %collective-permute-start.1 = (bf16[256,1024]{1,0:T(8,128)(2,1)}, bf16[256,1024]{1,0:T(8,128)(2,1)S(1)}, u32[]{:S(2)}, u32[]{:S(2)}) collective-permute-start(bf16[256,1024]{1,0:T(8,128)(2,1)} %get-tuple-element.35.qg0), channel_id=1, source_target_pairs={{0,8},{8,0},{1,9},{9,1},{2,10},{10,2},{3,11},{11,3},{4,12},{12,4},... | collective-permute-start | bytes 1572872 | tf_op jit(solution)/shard_map/ppermute | solution.py:323
  2.7 26.3 %collective-permute-start = (bf16[256,1024]{1,0:T(8,128)(2,1)}, bf16[256,1024]{1,0:T(8,128)(2,1)S(1)}, u32[]{:S(2)}, u32[]{:S(2)}) collective-permute-start(bf16[256,1024]{1,0:T(8,128)(2,1)} %get-tuple-element.35.qg0), channel_id=1, source_target_pairs={{0,16},{16,0},{1,17},{17,1},{2,18},{18,2},{3,19},{19,3},{4,20},{20... | collective-permute-start | bytes 1572872 | tf_op jit(solution)/shard_map/ppermute | solution.py:323
  6.0 11.0 %collective-permute-start.3 = (bf16[256,256]{1,0:T(8,128)(2,1)}, bf16[256,256]{1,0:T(8,128)(2,1)S(1)}, u32[]{:S(2)}, u32[]{:S(2)}) collective-permute-start(bf16[256,256]{1,0:T(8,128)(2,1)} %get-tuple-element.36.kv0), channel_id=1, source_target_pairs={{0,64},{32,96},{64,128},{96,160},{128,192},{160,224},{1,65},{33,97... | collective-permute-start | bytes 393224 | tf_op jit(solution)/shard_map/ppermute | solution.py:328
  11.5 12.9 %collective-permute-start.2 = (bf16[256,256]{1,0:T(8,128)(2,1)}, bf16[256,256]{1,0:T(8,128)(2,1)S(1)}, u32[]{:S(2)}, u32[]{:S(2)}) collective-permute-start(bf16[256,256]{1,0:T(8,128)(2,1)} %get-tuple-element.36.kv0), channel_id=1, source_target_pairs={{0,32},{32,64},{64,96},{96,128},{128,160},{160,192},{192,224},{1,3... | collective-permute-start | bytes 393224 | tf_op jit(solution)/shard_map/ppermute | solution.py:328
  14.4 14.5 %collective-permute-start.5 = (bf16[256,256]{1,0:T(8,128)(2,1)}, bf16[256,256]{1,0:T(8,128)(2,1)S(1)}, u32[]{:S(2)}, u32[]{:S(2)}) collective-permute-start(bf16[256,256]{1,0:T(8,128)(2,1)} %get-tuple-element.36.kv0), channel_id=1, source_target_pairs={{24,184},{56,216},{88,248},{25,185},{57,217},{89,249},{26,186},{58... | collective-permute-start | bytes 393224 | tf_op jit(solution)/shard_map/ppermute | solution.py:336
  17.0 12.0 %collective-permute-start.4 = (bf16[256,256]{1,0:T(8,128)(2,1)S(1)}, bf16[256,256]{1,0:T(8,128)(2,1)S(1)}, u32[]{:S(2)}, u32[]{:S(2)}) collective-permute-start(bf16[256,256]{1,0:T(8,128)(2,1)S(1)} %collective-permute-done.3.kv2), channel_id=1, source_target_pairs={{0,32},{32,64},{64,96},{96,128},{128,160},{160,192},{192,224},{1,3... | collective-permute-start | bytes 393224 | tf_op jit(solution)/shard_map/ppermute | solution.py:328
  24.4 1.0 %copy-start = (bf16[256,1024]{1,0:T(8,128)(2,1)S(1)}, bf16[256,1024]{1,0:T(8,128)(2,1)}, u32[]{:S(2)}) copy-start(bf16[256,1024]{1,0:T(8,128)(2,1)} %get-tuple-element.35.qg0) | copy-start | bytes 1572868
  25.5 0.9 copy-start.1
  26.4 0.7 copy-start.2
  29.0 3.4 %collective-permute-start.6 = (bf16[256,1024]{1,0:T(8,128)(2,1)S(1)}, bf16[256,1024]{1,0:T(8,128)(2,1)S(1)}, u32[]{:S(2)}, u32[]{:S(2)}) collective-permute-start(bf16[256,1024]{1,0:T(8,128)(2,1)S(1)} %collective-permute-done.qg2), channel_id=1, source_target_pairs={{0,8},{8,0},{1,9},{9,1},{2,10},{10,2},{3,11},{11,3},{4,12},{12,4},... | collective-permute-start | bytes 1572872 | tf_op jit(solution)/shard_map/ppermute | solution.py:323
  29.1 7.8 %collective-permute-start.7 = (bf16[256,256]{1,0:T(8,128)(2,1)S(1)}, bf16[256,256]{1,0:T(8,128)(2,1)S(1)}, u32[]{:S(2)}, u32[]{:S(2)}) collective-permute-start(bf16[256,256]{1,0:T(8,128)(2,1)S(1)} %collective-permute-done.4.kv3), channel_id=1, source_target_pairs={{0,32},{32,64},{64,96},{96,128},{128,160},{160,192},{192,224},{1,3... | collective-permute-start | bytes 393224 | tf_op jit(solution)/shard_map/ppermute | solution.py:328
  37.7 5.7 %collective-permute-start.9 = (f32[3,16,256]{2,1,0:T(8,128)S(1)}, f32[3,16,256]{2,1,0:T(8,128)S(1)}, u32[]{:S(2)}, u32[]{:S(2)}) collective-permute-start(f32[3,16,256]{2,1,0:T(8,128)S(1)} %get-tuple-element.45.st0), channel_id=1, source_target_pairs={{0,16},{16,0},{1,17},{17,1},{2,18},{18,2},{3,19},{19,3},{4,20},{20... | collective-permute-start | bytes 147464 | tf_op jit(solution)/shard_map/ppermute | solution.py:323
  39.3 4.1 %collective-permute-start.8 = (f32[3,16,256]{2,1,0:T(8,128)S(1)}, f32[3,16,256]{2,1,0:T(8,128)S(1)}, u32[]{:S(2)}, u32[]{:S(2)}) collective-permute-start(f32[3,16,256]{2,1,0:T(8,128)S(1)} %get-tuple-element.45.st0), channel_id=1, source_target_pairs={{0,8},{8,0},{1,9},{9,1},{2,10},{10,2},{3,11},{11,3},{4,12},{12,4},... | collective-permute-start | bytes 147464 | tf_op jit(solution)/shard_map/ppermute | solution.py:323
  43.4 1.2 %collective-permute-start.10 = (f32[3,16,256]{2,1,0:T(8,128)S(1)}, f32[3,16,256]{2,1,0:T(8,128)S(1)}, u32[]{:S(2)}, u32[]{:S(2)}) collective-permute-start(f32[3,16,256]{2,1,0:T(8,128)S(1)} %collective-permute-done.9.st2), channel_id=1, source_target_pairs={{0,8},{8,0},{1,9},{9,1},{2,10},{10,2},{3,11},{11,3},{4,12},{12,4},... | collective-permute-start | bytes 147464 | tf_op jit(solution)/shard_map/ppermute | solution.py:323
  48.8 12.5 %collective-permute-start.11 = (bf16[2,256,256]{2,1,0:T(8,128)(2,1)S(1)}, bf16[2,256,256]{2,1,0:T(8,128)(2,1)S(1)}, u32[]{:S(2)}, u32[]{:S(2)}) collective-permute-start(bf16[2,256,256]{2,1,0:T(8,128)(2,1)S(1)} %slice.12), channel_id=1, source_target_pairs={{64,0},{96,32},{128,64},{160,96},{192,128},{224,160},{65,1},{97,33... | collective-permute-start | bytes 786440 | tf_op jit(solution)/shard_map/ppermute | solution.py:328
  52.4 9.0 %collective-permute-start.12 = (bf16[256,512]{1,0:T(8,128)(2,1)S(1)}, bf16[256,512]{1,0:T(8,128)(2,1)S(1)}, u32[]{:S(2)}, u32[]{:S(2)}) collective-permute-start(bf16[256,512]{1,0:T(8,128)(2,1)S(1)} %get-tuple-element.53), channel_id=1, source_target_pairs={{0,8},{8,0},{1,9},{9,1},{2,10},{10,2},{3,11},{11,3},{4,12},{12,4},... | collective-permute-start | bytes 786440 | tf_op jit(solution)/shard_map/ppermute | solution.py:323
  52.6 22.0 %collective-permute-start.16 = (bf16[256,256]{1,0:T(8,128)(2,1)S(1)}, bf16[256,256]{1,0:T(8,128)(2,1)S(1)}, u32[]{:S(2)}, u32[]{:S(2)}) collective-permute-start(bf16[256,256]{1,0:T(8,128)(2,1)S(1)} %slice_bitcast_fusion), channel_id=1, source_target_pairs={{184,24},{216,56},{248,88},{185,25},{217,57},{249,89},{186,26},{21... | collective-permute-start | bytes 393224 | tf_op jit(solution)/shard_map/ppermute | solution.py:336
  61.4 21.2 %collective-permute-start.13 = (bf16[256,512]{1,0:T(8,128)(2,1)S(1)}, bf16[256,512]{1,0:T(8,128)(2,1)S(1)}, u32[]{:S(2)}, u32[]{:S(2)}) collective-permute-start(bf16[256,512]{1,0:T(8,128)(2,1)S(1)} %pair.1), channel_id=1, source_target_pairs={{0,16},{16,0},{1,17},{17,1},{2,18},{18,2},{3,19},{19,3},{4,20},{20... | collective-permute-start | bytes 786440 | tf_op jit(solution)/shard_map/ppermute | solution.py:323
  65.3 11.8 %collective-permute-start.15 = (bf16[256,256]{1,0:T(8,128)(2,1)S(1)}, bf16[256,256]{1,0:T(8,128)(2,1)S(1)}, u32[]{:S(2)}, u32[]{:S(2)}) collective-permute-start(bf16[256,256]{1,0:T(8,128)(2,1)S(1)} %get-tuple-element.67), channel_id=1, source_target_pairs={{64,0},{96,32},{128,64},{160,96},{192,128},{224,160},{65,1},{97,33... | collective-permute-start | bytes 393224 | tf_op jit(solution)/shard_map/ppermute | solution.py:328
  67.3 15.3 %collective-permute-start.14 = (bf16[256,256]{1,0:T(8,128)(2,1)S(1)}, bf16[256,256]{1,0:T(8,128)(2,1)S(1)}, u32[]{:S(2)}, u32[]{:S(2)}) collective-permute-start(bf16[256,256]{1,0:T(8,128)(2,1)S(1)} %get-tuple-element.68), channel_id=1, source_target_pairs={{32,0},{64,32},{96,64},{128,96},{160,128},{192,160},{224,192},{33,... | collective-permute-start | bytes 393224 | tf_op jit(solution)/shard_map/ppermute | solution.py:328
  82.6 1.5 %collective-permute-start.17 = (bf16[256,512]{1,0:T(8,128)(2,1)S(1)}, bf16[256,512]{1,0:T(8,128)(2,1)S(1)}, u32[]{:S(2)}, u32[]{:S(2)}) collective-permute-start(bf16[256,512]{1,0:T(8,128)(2,1)S(1)} %get-tuple-element.61), channel_id=1, source_target_pairs={{0,8},{8,0},{1,9},{9,1},{2,10},{10,2},{3,11},{11,3},{4,12},{12,4},... | collective-permute-start | bytes 786440 | tf_op jit(solution)/shard_map/ppermute | solution.py:323
